TPU v7x, 32 devices: a whole 2x2x4 slice. The times are simulated.
32 devices in a mesh: section: 2 (over core), dp: 16 (over z, y, x).
Axes of the slice: x: 2, y: 2, z: 4, core: 2. Of those that a mesh axis runs over, the one named last changes fastest.
Arguments:
- images: bfloat16 [4, 32, 8, 8, 512], P(None, 'dp'), may hold values from -6 to 6
- cotangent: bfloat16 [4, 32, 8, 8, 512], P(None, 'dp'), may hold values from -0.06591797 to 0.06591797
- counts: int32 [2], P('section'), may hold values from 1 to 4, as said below
- gains: float32 [8, 512], P('section'), may hold values from 0.1 to 1.9
- depthwise: float32 [8, 9, 512], P('section'), may hold values from -2 to 2
- pointwise: bfloat16 [8, 512, 512], P('section'), may hold values from -0.25 to 0.25
Outputs:
- grad_pointwise: float32 [8, 512, 512], P('section')
- grad_depthwise: float32 [8, 9, 512], P('section')
- grad_gains: float32 [8, 512], P('section')
Inputs may be any that keep to these rules, and one draw needn't show every extreme that they name: counts[s] is how many cells segment s applies, from its first slot on; at least one segment applies 4 cells.
All inputs are finite; a program needn't handle non-finite values.
Results may differ from a plain program's by a relative error of at most 0.0085.
Values may be sent and summed in bfloat16 or wider, within the bound.
A program may use at most 64 MiB of HBM per device.

v0:
```python
import functools

import jax
import jax.numpy as jnp
from jax import lax
from jax.experimental import pallas as pl
from jax.experimental.pallas import tpu as pltpu
from jax.sharding import PartitionSpec as P

MESH = pl.DeviceIdType.MESH
EPSILON = 1e-06
LANES = 128
TILE = 16
F32 = jnp.float32
BF16 = jnp.bfloat16
PACK_GAIN = 9
PACK_ACTIVE = 10


def kernel(
    plan,
    img,
    cot,
    pack_in,
    point_in,
    out,
    small_out,
    pack,
    point,
    xs,
    inv_all,
    normed_all,
    slope_all,
    act_all,
    gy,
    gl,
    taps,
    tap_acc,
    gain_acc,
    grads,
    reduced,
    from_core,
    small,
    small_recv,
    small_sum,
    send_sem,
    recv_sem,
    small_send,
    small_recv_sem,
    weight_send,
    weight_recv,
    load_sem,
    *landing,
):
    cells, slots, bits, halvings, height, image_rows, images = plan
    rows = images * image_rows
    channels = point.shape[-1]
    half = channels // 2
    blocks = channels // LANES
    core = lax.axis_index("section")
    me = lax.axis_index("dp")
    sibling = 1 - core

    digits = [lax.rem(me // (1 << b), 2) for b in range(bits)]
    weights = [1 << b for b in range(bits)]
    if bits >= 2:
        first, second = digits[0], digits[1]
        digits[0] = first + core * (second - first)
        digits[1] = second + core * (first - second)
        weights[0] = 1 + core
        weights[1] = 2 - core
    partners = [me + (1 - 2 * d) * w for d, w in zip(digits, weights)]
    base = core * half

    barrier = pltpu.get_barrier_semaphore()
    pl.semaphore_signal(barrier, inc=1, device_id=(sibling, me), device_id_type=MESH)
    for partner in partners:
        pl.semaphore_signal(barrier, inc=1, device_id=(core, partner), device_id_type=MESH)

    load_img = pltpu.make_async_copy(img.at[core], xs.at[0], load_sem.at[0])
    load_cot = pltpu.make_async_copy(cot.at[core], gy, load_sem.at[1])
    load_pack = pltpu.make_async_copy(pack_in, pack.at[pl.ds(core * cells, cells)], load_sem.at[2])
    load_img.start()
    load_pack.start()
    for j in range(cells):
        pltpu.make_async_copy(
            point_in.at[j], point.at[core * cells + j], weight_recv.at[core * cells + j]
        ).start()
    load_cot.start()
    pl.semaphore_wait(barrier, 1 + bits)

    def pack_copy():
        return pltpu.make_async_remote_copy(
            src_ref=pack_in,
            dst_ref=pack.at[pl.ds(core * cells, cells)],
            send_sem=load_sem.at[3],
            recv_sem=load_sem.at[4],
            device_id=(sibling, me),
            device_id_type=MESH,
        )

    def point_copy(j):
        return pltpu.make_async_remote_copy(
            src_ref=point_in.at[j],
            dst_ref=point.at[core * cells + j],
            send_sem=weight_send.at[j],
            recv_sem=weight_recv.at[core * cells + j],
            device_id=(sibling, me),
            device_id_type=MESH,
        )

    pack_copy().start()
    for j in range(cells):
        point_copy(j).start()
    load_img.wait()
    load_pack.wait()
    pack_copy().wait()

    column = lax.broadcasted_iota(jnp.int32, (8, channels), 0)

    def set_taps(k, low_tap_edge, high_tap_edge):
        for p in range(3):
            for q in range(3):
                t = p * 3 + q
                tile = jnp.broadcast_to(pack[k, t : t + 1, :], (8, channels))
                if q == 0:
                    tile = jnp.where(column == low_tap_edge, 0.0, tile)
                if q == 2:
                    tile = jnp.where(column == high_tap_edge, 0.0, tile)
                taps[t] = tile

    def lane(block):
        return slice(block * LANES, (block + 1) * LANES)

    def row_of(k, row, block, count):
        return jnp.broadcast_to(pack[k, row : row + 1, lane(block)], (count, LANES))

    def forward(k, carry):
        pltpu.make_async_copy(point.at[k], point.at[k], weight_recv.at[k]).wait()
        set_taps(k, 0, 7)

        def image(i, carry):
            at = pl.ds(pl.multiple_of(i * image_rows, image_rows), image_rows)
            xl = [xs[k, at, lane(b)].astype(F32) for b in range(blocks)]
            squares = sum(x * x for x in xl)
            mean = jnp.sum(squares, axis=1, keepdims=True) * (1.0 / channels)
            inv = jnp.broadcast_to(lax.rsqrt(mean + EPSILON), (image_rows, LANES))
            inv_all[k, at, :] = inv
            for b in range(blocks):
                normed = xl[b] * inv * row_of(k, PACK_GAIN, b, image_rows)
                normed_all[k, at, lane(b)] = normed
                mid = [normed[8 * h : 8 * h + 8] for h in range(height)]
                moved = [
                    [pltpu.roll(m, 1, axis=0) for m in mid],
                    mid,
                    [pltpu.roll(m, 7, axis=0) for m in mid],
                ]
                w = [taps[t, :, lane(b)] for t in range(9)]
                linear = []
                for h in range(height):
                    total = None
                    for p in range(3):
                        if 0 <= h + p - 1 < height:
                            for q in range(3):
                                term = w[p * 3 + q] * moved[q][h + p - 1]
                                total = term if total is None else total + term
                    linear.append(total)
                linear = jnp.concatenate(linear, axis=0)
                sigma = 0.5 * jnp.tanh(0.5 * linear) + 0.5
                act = linear * sigma
                act_all[k, at, lane(b)] = act.astype(BF16)
                slope_all[k, at, lane(b)] = sigma + act * (1.0 - sigma)
            return carry

        lax.fori_loop(0, images, image, 0)
        mixed = jnp.dot(act_all[k], point[k], preferred_element_type=F32)
        x = xs[k]
        y = (x.astype(F32) + mixed).astype(BF16)
        active = jnp.broadcast_to(pack[k, PACK_ACTIVE : PACK_ACTIVE + 1, :], (rows, channels))
        xs[k + 1] = jnp.where(active > 0.5, y.astype(F32), x.astype(F32)).astype(BF16)
        return carry

    lax.fori_loop(0, slots, forward, 0)
    load_cot.wait()
    for j in range(cells):
        point_copy(j).wait_send()

    def remote(src, dst, k, step, device):
        return pltpu.make_async_remote_copy(
            src_ref=src,
            dst_ref=dst,
            send_sem=send_sem.at[k, step],
            recv_sem=recv_sem.at[k, step],
            device_id=device,
            device_id_type=MESH,
        )

    def span(start, size):
        return pl.ds(pl.multiple_of(start, TILE), size)

    keep, away, sizes = [], [], []
    offset, size = base, half
    for b in range(bits):
        if b < halvings:
            size = size // 2
            away.append(offset + (1 - digits[b]) * size)
            offset = offset + digits[b] * size
        else:
            away.append(offset)
        keep.append(offset)
        sizes.append(size)

    def core_copy(k):
        return remote(
            grads.at[k, span(sibling * half, half)], from_core.at[k], k, 0, (sibling, me)
        )

    def scatter_copy(k, b):
        return remote(
            grads.at[k, span(away[b], sizes[b])], landing[b].at[k], k, 1 + b, (core, partners[b])
        )

    def gather_copy(k, b):
        part = span(keep[b], sizes[b])
        return remote(
            reduced.at[k, part], reduced.at[k, part], k, 1 + bits + b, (core, partners[b])
        )

    def home_copy(k):
        part = span(base, half)
        return remote(
            reduced.at[k, part],
            out.at[lax.rem(k, cells), part],
            k,
            1 + bits + halvings,
            (sibling, me),
        )

    def add_landed(k, part, landed):
        grads[k, part] = (grads[k, part].astype(F32) + landed.astype(F32)).astype(BF16)

    def finish(k):
        part = span(base, half)

        @pl.when(core != k // cells)
        def _():
            home_copy(k).start()

        @pl.when(core == k // cells)
        def _():
            out[lax.rem(k, cells), part] = reduced[k, part]

    def stage(k, age):
        if age <= 1 + bits:
            if age == 1:
                core_copy(k).wait()
                add_landed(k, span(base, half), from_core[k])
            else:
                b = age - 2
                scatter_copy(k, b).wait()
                add_landed(k, span(keep[b], sizes[b]), landing[b][k])
            if age <= bits:
                scatter_copy(k, age - 1).start()
            else:
                part = span(offset, size)
                reduced[k, part] = grads[k, part]
                if halvings:
                    gather_copy(k, halvings - 1).start()
                else:
                    finish(k)
        elif age <= 1 + bits + halvings:
            b = halvings - (age - 1 - bits)
            gather_copy(k, b).wait()
            if b > 0:
                gather_copy(k, b - 1).start()
            else:
                finish(k)
        else:

            @pl.when(core != k // cells)
            def _():
                home_copy(k).wait_send()

            @pl.when(core == k // cells)
            def _():
                home_copy(k).wait_recv()

    last_age = 2 + bits + halvings

    def small_copy(step):
        if step == 0:
            src, device = small.at[sibling], (sibling, me)
        else:
            src, device = small_sum.at[step - 1], (core, partners[step - 1])
        return pltpu.make_async_remote_copy(
            src_ref=src,
            dst_ref=small_recv.at[step],
            send_sem=small_send.at[step],
            recv_sem=small_recv_sem.at[step],
            device_id=device,
            device_id_type=MESH,
        )

    def small_stage(age):
        small_copy(age - 1).wait()
        own = small[core] if age == 1 else small_sum[age - 2]
        total = own + small_recv[age - 1]
        if age <= bits:
            small_sum[age - 1] = total
            small_copy(age).start()
        else:
            small_out[...] = total

    def backward(k):
        active = jnp.broadcast_to(
            pack[k, PACK_ACTIVE : PACK_ACTIVE + 1, :], (channels, channels)
        )
        gp = lax.dot_general(
            act_all[k], gy[...], (((0,), (0,)), ((), ())), preferred_element_type=F32
        )
        grads[k] = jnp.where(active > 0.5, gp, 0.0).astype(BF16)
        core_copy(k).start()
        ga = lax.dot_general(
            gy[...], point[k], (((1,), (1,)), ((), ())), preferred_element_type=F32
        )
        gl[...] = ga * slope_all[k]
        set_taps(k, 7, 0)
        tap_acc[...] = jnp.zeros_like(tap_acc)
        gain_acc[...] = jnp.zeros_like(gain_acc)

        def image(i, carry):
            at = pl.ds(pl.multiple_of(i * image_rows, image_rows), image_rows)
            inv = inv_all[k, at, :]
            gns = []
            for b in range(blocks):
                mid = [
                    gl[pl.ds(pl.multiple_of(i * image_rows + 8 * h, 8), 8), lane(b)]
                    for h in range(height)
                ]
                n = [
                    normed_all[
                        k, pl.ds(pl.multiple_of(i * image_rows + 8 * h, 8), 8), lane(b)
                    ]
                    for h in range(height)
                ]
                moved = [
                    [pltpu.roll(m, 7, axis=0) for m in mid],
                    mid,
                    [pltpu.roll(m, 1, axis=0) for m in mid],
                ]
                gn = [None] * height
                for p in range(3):
                    for q in range(3):
                        t = p * 3 + q
                        w = taps[t, :, lane(b)]
                        acc = tap_acc[t, :, lane(b)]
                        for h in range(height):
                            if 0 <= h - p + 1 < height:
                                piece = moved[q][h - p + 1]
                                term = w * piece
                                gn[h] = term if gn[h] is None else gn[h] + term
                                acc = acc + n[h] * piece
                        tap_acc[t, :, lane(b)] = acc
                gns.append(jnp.concatenate(gn, axis=0))
            dots = None
            us, xl = [], []
            for b in range(blocks):
                x = xs[k, at, lane(b)].astype(F32)
                term = gns[b] * x * inv
                gain_acc[:, lane(b)] += sum(term[8 * h : 8 * h + 8] for h in range(height))
                u = gns[b] * row_of(k, PACK_GAIN, b, image_rows)
                us.append(u)
                xl.append(x)
                dots = u * x if dots is None else dots + u * x
            mean = jnp.sum(dots, axis=1, keepdims=True) * (1.0 / channels)
            fall = jnp.broadcast_to(mean, (image_rows, LANES)) * (inv * inv * inv)
            for b in range(blocks):
                g = gy[at, lane(b)].astype(F32)
                gx = g + inv * us[b] - xl[b] * fall
                on = row_of(k, PACK_ACTIVE, b, image_rows) > 0.5
                gy[at, lane(b)] = jnp.where(on, gx, g).astype(BF16)
            return carry

        lax.fori_loop(0, images, image, 0)

        section, j = k // cells, lax.rem(k, cells)
        on = pack[k, PACK_ACTIVE : PACK_ACTIVE + 1, :] > 0.5
        sums = []
        for t in range(9):
            tile = tap_acc[t]
            if t % 3 == 0:
                tile = jnp.where(column == 7, 0.0, tile)
            if t % 3 == 2:
                tile = jnp.where(column == 0, 0.0, tile)
            sums.append(jnp.where(on, jnp.sum(tile, axis=0, keepdims=True), 0.0))
        gain = jnp.where(on, jnp.sum(gain_acc[...], axis=0, keepdims=True), 0.0)
        for t in range(8):
            small[section, j, t : t + 1, :] = sums[t]
        small[section, cells, pl.ds(j, 1), :] = sums[8]
        small[section, cells, pl.ds(cells + j, 1), :] = gain

    def tick(t, carry):
        for age in reversed(range(1, last_age + 1)):

            @pl.when((t >= age) & (t < age + slots))
            def _(age=age):
                stage(slots - 1 - (t - age), age)

        for age in range(1, bits + 2):

            @pl.when(t == slots - 1 + age)
            def _(age=age):
                small_stage(age)

        @pl.when(t < slots)
        def _():
            backward(slots - 1 - t)

        @pl.when(t == slots - 1)
        def _():
            small_copy(0).start()

        return carry

    lax.fori_loop(0, slots + last_age, tick, 0)


def local(images, cotangent, counts, gains, depthwise, pointwise):
    cells, channels = gains.shape
    sections = lax.axis_size("section")
    slots = sections * cells
    replicas = lax.axis_size("dp")
    bits = replicas.bit_length() - 1
    assert sections == 2 and replicas == 1 << bits and cells == 4
    micro, batch, height, width = images.shape[:4]
    assert width == 8 and depthwise.shape[1] == 9
    image_rows = height * width
    per_core = micro * batch // 2
    rows = per_core * image_rows
    half = channels // 2
    halvings = 0
    while halvings < bits and (half >> (halvings + 1)) % TILE == 0 and (half >> (halvings + 1)):
        halvings += 1

    img = images.reshape(2, rows, channels)
    cot = cotangent.reshape(2, rows, channels)
    active = (jnp.arange(cells) < counts[0]).astype(F32)[:, None, None]
    pack = jnp.concatenate(
        [
            depthwise,
            gains[:, None, :],
            jnp.broadcast_to(active, (cells, 1, channels)),
            jnp.zeros((cells, 5, channels), F32),
        ],
        axis=1,
    )
    landing = [
        pltpu.VMEM((slots, half >> min(b + 1, halvings), channels), BF16) for b in range(bits)
    ]
    steps = 2 + bits + halvings
    plan = (cells, slots, bits, halvings, height, image_rows, per_core)
    grid_rows = (cells + 1, 8, channels)
    moved, small = pl.pallas_call(
        functools.partial(kernel, plan),
        out_shape=(
            jax.ShapeDtypeStruct((cells, channels, channels), BF16),
            jax.ShapeDtypeStruct(grid_rows, F32),
        ),
        in_specs=[pl.BlockSpec(memory_space=pl.ANY)] * 4,
        out_specs=(
            pl.BlockSpec(memory_space=pltpu.VMEM),
            pl.BlockSpec(memory_space=pltpu.VMEM),
        ),
        scratch_shapes=[
            pltpu.VMEM((slots, 16, channels), F32),
            pltpu.VMEM((slots, channels, channels), BF16),
            pltpu.VMEM((slots + 1, rows, channels), BF16),
            pltpu.VMEM((slots, rows, LANES), F32),
            pltpu.VMEM((slots, rows, channels), F32),
            pltpu.VMEM((slots, rows, channels), F32),
            pltpu.VMEM((slots, rows, channels), BF16),
            pltpu.VMEM((rows, channels), BF16),
            pltpu.VMEM((rows, channels), F32),
            pltpu.VMEM((9, 8, channels), F32),
            pltpu.VMEM((9, 8, channels), F32),
            pltpu.VMEM((8, channels), F32),
            pltpu.VMEM((slots, channels, channels), BF16),
            pltpu.VMEM((slots, channels, channels), BF16),
            pltpu.VMEM((slots, half, channels), BF16),
            pltpu.VMEM((2,) + grid_rows, F32),
            pltpu.VMEM((bits + 1,) + grid_rows, F32),
            pltpu.VMEM((max(bits, 1),) + grid_rows, F32),
            pltpu.SemaphoreType.DMA((slots, steps)),
            pltpu.SemaphoreType.DMA((slots, steps)),
            pltpu.SemaphoreType.DMA((bits + 1,)),
            pltpu.SemaphoreType.DMA((bits + 1,)),
            pltpu.SemaphoreType.DMA((cells,)),
            pltpu.SemaphoreType.DMA((slots,)),
            pltpu.SemaphoreType.DMA((5,)),
        ]
        + landing,
        compiler_params=pltpu.CompilerParams(
            collective_id=0, has_side_effects=True, vmem_limit_bytes=56 * 1024 * 1024
        ),
    )(img, cot, pack, pointwise)
    depth = jnp.concatenate([small[:cells], small[cells, :cells][:, None, :]], axis=1)
    return (moved.astype(F32), depth, small[cells, cells:])


def solution(mesh):
    placed = (
        P(None, "dp", None, None, None),
        P(None, "dp", None, None, None),
        P("section"),
        P("section", None),
        P("section", None, None),
        P("section", None, None),
    )
    return jax.shard_map(
        local,
        mesh=mesh,
        in_specs=placed,
        out_specs=(P("section", None, None), P("section", None, None), P("section", None)),
        check_vma=False,
    )
```

profile of v0, /device:TPU:0, one launch (start us, length us, event | category | flops | bytes accessed | tf_op | source)
XLA Modules:
  0.0 96.1 jit_solution(13992768984041632728)
XLA Ops:
  1.3 0.1 pad.5.clone
  1.4 0.1 broadcast_in_dim.13
  1.4 0.7 broadcast_in_dim.12
  2.1 0.9 copy.9
  3.1 0.7 maximum_maximum_fusion.pack_in
  3.8 85.2 %shard_map.85 = (bf16[4,512,512]{2,1,0:T(8,128)(2,1)}, f32[5,8,512]{2,1,0:T(8,128)}) custom-call(bf16[2,256,512]{2,1,0:T(8,128)(2,1)} %bitcast.8, bf16[2,256,512]{2,1,0:T(8,128)(2,1)} %bitcast.9, f32[4,16,512]{2,1,0:T(8,128)} %maximum_maximum_fusion.pack_in, bf16[4,512,512]{2,1,0:T(8,128)(2,1)} %point_in.1), custom_call_target="tpu_custom_call" | custom-call | tf_op jit(solution)/shard_map/pallas_call | solution.py:463
  89.0 1.4 %slice_bitcast_fusion = (f32[4,512]{1,0:T(4,128)}, f32[4,1,512]{2,0,1:T(4,128)S(1)}) fusion(f32[5,8,512]{2,1,0:T(8,128)} %get-tuple-element.6), kind=kLoop, calls=%fused_computation.2 | loop fusion | bytes 32768 | tf_op jit(solution)/shard_map/squeeze | solution.py:507
  90.4 0.8 slice.9
  91.2 0.7 copy.11
  91.9 4.2 %convert_element_type.11 = f32[4,512,512]{2,1,0:T(8,128)} convert(bf16[4,512,512]{2,1,0:T(8,128)(2,1)} %get-tuple-element.5) | non-fusion elementwise | flops 1048576 | bytes 6291456 | tf_op jit(solution)/shard_map/convert_element_type | solution.py:507
  (4 shorter events, 0.0 us)
where the time goes:
time: 96.5 us; the launch traced here: 96.1 us
  Pallas kernels  85.2 us (88%)
  other arithmetic  4.94 us (5%)
  local copies, waits for them, and re-layouts  4.7 us (5%)
  between operations  1.32 us (1%)
    pallas_call x1, Pallas kernels, local(): pl.pallas_call(functools.partial(kernel, plan), out_shape=(jax.ShapeDtype...  85.2 us
    convert_element_type x1, other arithmetic, local(): return (moved.astype(F32), depth, small[cells, cells:])  4.19 us

commit v1 on v0

--- a/solution.py
+++ b/solution.py
@@ -13,19 +13,20 @@
 TILE = 16
 F32 = jnp.float32
 BF16 = jnp.bfloat16
-PACK_GAIN = 9
-PACK_ACTIVE = 10
 
 
 def kernel(
     plan,
     img,
     cot,
-    pack_in,
+    counts,
+    gains,
+    depth_in,
     point_in,
     out,
     small_out,
-    pack,
+    depth,
+    meta,
     point,
     xs,
     inv_all,
@@ -52,7 +53,8 @@
     load_sem,
     *landing,
 ):
-    cells, slots, bits, halvings, height, image_rows, images = plan
+    cells, used, masked, bits, halvings, height, image_rows, images = plan
+    slots = sum(used)
     rows = images * image_rows
     channels = point.shape[-1]
     half = channels // 2
@@ -60,6 +62,10 @@
     core = lax.axis_index("section")
     me = lax.axis_index("dp")
     sibling = 1 - core
+
+    def owner(k):
+        segment = (k + 8 - used[0]) // 8
+        return segment, k - segment * used[0]
 
     digits = [lax.rem(me // (1 << b), 2) for b in range(bits)]
     weights = [1 << b for b in range(bits)]
@@ -79,61 +85,93 @@
 
     load_img = pltpu.make_async_copy(img.at[core], xs.at[0], load_sem.at[0])
     load_cot = pltpu.make_async_copy(cot.at[core], gy, load_sem.at[1])
-    load_pack = pltpu.make_async_copy(pack_in, pack.at[pl.ds(core * cells, cells)], load_sem.at[2])
+    load_depth = pltpu.make_async_copy(
+        depth_in, depth.at[pl.ds(core * cells, cells)], load_sem.at[2]
+    )
     load_img.start()
-    load_pack.start()
+    load_depth.start()
+
+    def place(j):
+        return core * used[0] + j
+
+    def point_load(j):
+        return pltpu.make_async_copy(
+            point_in.at[j], point.at[place(j)], weight_recv.at[place(j)]
+        )
+
+    def each_cell(act):
+        for j in range(cells):
+            if j < min(used):
+                act(j)
+            elif j < max(used):
+
+                @pl.when(core == (0 if used[0] > used[1] else 1))
+                def _(j=j):
+                    act(j)
+
+    each_cell(lambda j: point_load(j).start())
+    load_cot.start()
     for j in range(cells):
-        pltpu.make_async_copy(
-            point_in.at[j], point.at[core * cells + j], weight_recv.at[core * cells + j]
-        ).start()
-    load_cot.start()
+        meta[core, j : j + 1, :] = gains[j : j + 1, :]
+        meta[core, cells + j : cells + j + 1, :] = jnp.where(
+            jnp.full((1, channels), j, jnp.int32) < counts[0], 1.0, 0.0
+        )
     pl.semaphore_wait(barrier, 1 + bits)
 
-    def pack_copy():
+    def to_sibling(src, dst, send, recv):
         return pltpu.make_async_remote_copy(
-            src_ref=pack_in,
-            dst_ref=pack.at[pl.ds(core * cells, cells)],
-            send_sem=load_sem.at[3],
-            recv_sem=load_sem.at[4],
+            src_ref=src,
+            dst_ref=dst,
+            send_sem=send,
+            recv_sem=recv,
             device_id=(sibling, me),
             device_id_type=MESH,
         )
 
+    def depth_copy():
+        return to_sibling(
+            depth_in, depth.at[pl.ds(core * cells, cells)], load_sem.at[3], load_sem.at[4]
+        )
+
+    def meta_copy():
+        return to_sibling(meta.at[core], meta.at[core], load_sem.at[5], load_sem.at[6])
+
     def point_copy(j):
-        return pltpu.make_async_remote_copy(
-            src_ref=point_in.at[j],
-            dst_ref=point.at[core * cells + j],
-            send_sem=weight_send.at[j],
-            recv_sem=weight_recv.at[core * cells + j],
-            device_id=(sibling, me),
-            device_id_type=MESH,
-        )
-
-    pack_copy().start()
-    for j in range(cells):
-        point_copy(j).start()
+        return to_sibling(
+            point_in.at[j], point.at[place(j)], weight_send.at[j], weight_recv.at[place(j)]
+        )
+
+    depth_copy().start()
+    meta_copy().start()
+    each_cell(lambda j: point_copy(j).start())
     load_img.wait()
-    load_pack.wait()
-    pack_copy().wait()
+    load_depth.wait()
+    depth_copy().wait()
+    meta_copy().wait()
 
     column = lax.broadcasted_iota(jnp.int32, (8, channels), 0)
 
     def set_taps(k, low_tap_edge, high_tap_edge):
+        segment, j = owner(k)
         for p in range(3):
             for q in range(3):
                 t = p * 3 + q
-                tile = jnp.broadcast_to(pack[k, t : t + 1, :], (8, channels))
+                tile = jnp.broadcast_to(
+                    depth[segment * cells + j, t : t + 1, :], (8, channels)
+                )
                 if q == 0:
                     tile = jnp.where(column == low_tap_edge, 0.0, tile)
                 if q == 2:
                     tile = jnp.where(column == high_tap_edge, 0.0, tile)
                 taps[t] = tile
+        taps[9] = jnp.broadcast_to(meta[segment, pl.ds(j, 1), :], (8, channels))
+        taps[10] = jnp.broadcast_to(meta[segment, pl.ds(cells + j, 1), :], (8, channels))
 
     def lane(block):
         return slice(block * LANES, (block + 1) * LANES)
 
-    def row_of(k, row, block, count):
-        return jnp.broadcast_to(pack[k, row : row + 1, lane(block)], (count, LANES))
+    def stacked(tile, count):
+        return jnp.concatenate([tile] * (count // 8), axis=0)
 
     def forward(k, carry):
         pltpu.make_async_copy(point.at[k], point.at[k], weight_recv.at[k]).wait()
@@ -147,7 +185,7 @@
             inv = jnp.broadcast_to(lax.rsqrt(mean + EPSILON), (image_rows, LANES))
             inv_all[k, at, :] = inv
             for b in range(blocks):
-                normed = xl[b] * inv * row_of(k, PACK_GAIN, b, image_rows)
+                normed = xl[b] * inv * stacked(taps[9, :, lane(b)], image_rows)
                 normed_all[k, at, lane(b)] = normed
                 mid = [normed[8 * h : 8 * h + 8] for h in range(height)]
                 moved = [
@@ -174,16 +212,16 @@
 
         lax.fori_loop(0, images, image, 0)
         mixed = jnp.dot(act_all[k], point[k], preferred_element_type=F32)
-        x = xs[k]
-        y = (x.astype(F32) + mixed).astype(BF16)
-        active = jnp.broadcast_to(pack[k, PACK_ACTIVE : PACK_ACTIVE + 1, :], (rows, channels))
-        xs[k + 1] = jnp.where(active > 0.5, y.astype(F32), x.astype(F32)).astype(BF16)
+        x = xs[k].astype(F32)
+        y = x + mixed
+        if masked:
+            y = jnp.where(stacked(taps[10], rows) > 0.5, y, x)
+        xs[k + 1] = y.astype(BF16)
         return carry
 
     lax.fori_loop(0, slots, forward, 0)
     load_cot.wait()
-    for j in range(cells):
-        point_copy(j).wait_send()
+    each_cell(lambda j: point_copy(j).wait_send())
 
     def remote(src, dst, k, step, device):
         return pltpu.make_async_remote_copy(
@@ -230,7 +268,7 @@
         part = span(base, half)
         return remote(
             reduced.at[k, part],
-            out.at[lax.rem(k, cells), part],
+            out.at[owner(k)[1], part],
             k,
             1 + bits + halvings,
             (sibling, me),
@@ -241,51 +279,50 @@
 
     def finish(k):
         part = span(base, half)
-
-        @pl.when(core != k // cells)
+        segment, j = owner(k)
+
+        @pl.when(core != segment)
         def _():
             home_copy(k).start()
 
-        @pl.when(core == k // cells)
+        @pl.when(core == segment)
         def _():
-            out[lax.rem(k, cells), part] = reduced[k, part]
+            out[j, part] = reduced[k, part]
 
     def stage(k, age):
-        if age <= 1 + bits:
-            if age == 1:
-                core_copy(k).wait()
-                add_landed(k, span(base, half), from_core[k])
-            else:
-                b = age - 2
-                scatter_copy(k, b).wait()
-                add_landed(k, span(keep[b], sizes[b]), landing[b][k])
-            if age <= bits:
-                scatter_copy(k, age - 1).start()
+        if age <= bits:
+            b = age - 1
+            scatter_copy(k, b).wait()
+            add_landed(k, span(keep[b], sizes[b]), landing[b][k])
+            if age < bits:
+                scatter_copy(k, age).start()
             else:
                 part = span(offset, size)
                 reduced[k, part] = grads[k, part]
-                if halvings:
-                    gather_copy(k, halvings - 1).start()
-                else:
-                    finish(k)
-        elif age <= 1 + bits + halvings:
-            b = halvings - (age - 1 - bits)
+                gather_copy(k, halvings - 1).start()
+        else:
+            b = halvings - (age - bits)
             gather_copy(k, b).wait()
             if b > 0:
                 gather_copy(k, b - 1).start()
             else:
                 finish(k)
-        else:
-
-            @pl.when(core != k // cells)
-            def _():
-                home_copy(k).wait_send()
-
-            @pl.when(core == k // cells)
-            def _():
-                home_copy(k).wait_recv()
-
-    last_age = 2 + bits + halvings
+
+    last_age = bits + halvings
+
+    def pump(n, middle):
+        ages = [a for a in range(1, last_age + 1) if a % 2 == (1 if middle else 0)]
+        ages.sort(key=lambda a: sizes_of[a])
+        for age in ages:
+            turn = (age + 1) // 2 if middle else 1 + age // 2
+
+            @pl.when((n >= turn) & (n < turn + slots))
+            def _(age=age, turn=turn):
+                stage(slots - 1 - (n - turn), age)
+
+    sizes_of = {}
+    for a in range(1, last_age + 1):
+        sizes_of[a] = sizes[a - 1] if a <= bits else sizes[halvings - (a - bits)]
 
     def small_copy(step):
         if step == 0:
@@ -311,22 +348,31 @@
         else:
             small_out[...] = total
 
-    def backward(k):
-        active = jnp.broadcast_to(
-            pack[k, PACK_ACTIVE : PACK_ACTIVE + 1, :], (channels, channels)
-        )
+    small[...] = jnp.zeros_like(small)
+    for j in range(cells):
+        if j >= min(used):
+
+            @pl.when(core == (0 if used[0] < used[1] else 1))
+            def _(j=j):
+                out[j] = jnp.zeros((channels, channels), BF16)
+
+    def backward(n):
+        k = slots - 1 - n
         gp = lax.dot_general(
             act_all[k], gy[...], (((0,), (0,)), ((), ())), preferred_element_type=F32
         )
-        grads[k] = jnp.where(active > 0.5, gp, 0.0).astype(BF16)
+        set_taps(k, 7, 0)
+        if masked:
+            gp = jnp.where(stacked(taps[10], channels) > 0.5, gp, 0.0)
+        grads[k] = gp.astype(BF16)
         core_copy(k).start()
         ga = lax.dot_general(
             gy[...], point[k], (((1,), (1,)), ((), ())), preferred_element_type=F32
         )
         gl[...] = ga * slope_all[k]
-        set_taps(k, 7, 0)
         tap_acc[...] = jnp.zeros_like(tap_acc)
         gain_acc[...] = jnp.zeros_like(gain_acc)
+        pump(n, True)
 
         def image(i, carry):
             at = pl.ds(pl.multiple_of(i * image_rows, image_rows), image_rows)
@@ -337,7 +383,7 @@
                     gl[pl.ds(pl.multiple_of(i * image_rows + 8 * h, 8), 8), lane(b)]
                     for h in range(height)
                 ]
-                n = [
+                tiles = [
                     normed_all[
                         k, pl.ds(pl.multiple_of(i * image_rows + 8 * h, 8), 8), lane(b)
                     ]
@@ -359,7 +405,7 @@
                                 piece = moved[q][h - p + 1]
                                 term = w * piece
                                 gn[h] = term if gn[h] is None else gn[h] + term
-                                acc = acc + n[h] * piece
+                                acc = acc + tiles[h] * piece
                         tap_acc[t, :, lane(b)] = acc
                 gns.append(jnp.concatenate(gn, axis=0))
             dots = None
@@ -368,7 +414,7 @@
                 x = xs[k, at, lane(b)].astype(F32)
                 term = gns[b] * x * inv
                 gain_acc[:, lane(b)] += sum(term[8 * h : 8 * h + 8] for h in range(height))
-                u = gns[b] * row_of(k, PACK_GAIN, b, image_rows)
+                u = gns[b] * stacked(taps[9, :, lane(b)], image_rows)
                 us.append(u)
                 xl.append(x)
                 dots = u * x if dots is None else dots + u * x
@@ -377,14 +423,18 @@
             for b in range(blocks):
                 g = gy[at, lane(b)].astype(F32)
                 gx = g + inv * us[b] - xl[b] * fall
-                on = row_of(k, PACK_ACTIVE, b, image_rows) > 0.5
-                gy[at, lane(b)] = jnp.where(on, gx, g).astype(BF16)
+                if masked:
+                    gx = jnp.where(stacked(taps[10, :, lane(b)], image_rows) > 0.5, gx, g)
+                gy[at, lane(b)] = gx.astype(BF16)
             return carry
 
         lax.fori_loop(0, images, image, 0)
-
-        section, j = k // cells, lax.rem(k, cells)
-        on = pack[k, PACK_ACTIVE : PACK_ACTIVE + 1, :] > 0.5
+        core_copy(k).wait()
+        add_landed(k, span(base, half), from_core[k])
+        scatter_copy(k, 0).start()
+
+        segment, j = owner(k)
+        on = taps[10, 0:1, :] > 0.5
         sums = []
         for t in range(9):
             tile = tap_acc[t]
@@ -392,43 +442,73 @@
                 tile = jnp.where(column == 7, 0.0, tile)
             if t % 3 == 2:
                 tile = jnp.where(column == 0, 0.0, tile)
-            sums.append(jnp.where(on, jnp.sum(tile, axis=0, keepdims=True), 0.0))
-        gain = jnp.where(on, jnp.sum(gain_acc[...], axis=0, keepdims=True), 0.0)
+            total = jnp.sum(tile, axis=0, keepdims=True)
+            sums.append(jnp.where(on, total, 0.0) if masked else total)
+        gain = jnp.sum(gain_acc[...], axis=0, keepdims=True)
+        if masked:
+            gain = jnp.where(on, gain, 0.0)
         for t in range(8):
-            small[section, j, t : t + 1, :] = sums[t]
-        small[section, cells, pl.ds(j, 1), :] = sums[8]
-        small[section, cells, pl.ds(cells + j, 1), :] = gain
-
-    def tick(t, carry):
-        for age in reversed(range(1, last_age + 1)):
-
-            @pl.when((t >= age) & (t < age + slots))
-            def _(age=age):
-                stage(slots - 1 - (t - age), age)
+            small[segment, j, t : t + 1, :] = sums[t]
+        small[segment, cells, pl.ds(j, 1), :] = sums[8]
+        small[segment, cells, pl.ds(cells + j, 1), :] = gain
+
+    def turn(n, carry):
+        pump(n, False)
+
+        @pl.when(n < slots)
+        def _():
+            backward(n)
+
+        @pl.when(n >= slots)
+        def _():
+            pump(n, True)
+
+        @pl.when(n == slots - 1)
+        def _():
+            small_copy(0).start()
 
         for age in range(1, bits + 2):
 
-            @pl.when(t == slots - 1 + age)
+            @pl.when(n == slots + (age - 1) // 2)
             def _(age=age):
                 small_stage(age)
 
-        @pl.when(t < slots)
+        return carry
+
+    lax.fori_loop(0, slots + 1 + max(last_age // 2, (bits + 2) // 2), turn, 0)
+
+    def wait_home(n, carry):
+        k = slots - 1 - n
+        segment, _ = owner(k)
+
+        @pl.when(core != segment)
         def _():
-            backward(slots - 1 - t)
-
-        @pl.when(t == slots - 1)
+            home_copy(k).wait_send()
+
+        @pl.when(core == segment)
         def _():
-            small_copy(0).start()
+            home_copy(k).wait_recv()
 
         return carry
 
-    lax.fori_loop(0, slots + last_age, tick, 0)
+    lax.fori_loop(0, slots, wait_home, 0)
+
+
+def widen(moved, small, point_out, depth_out, gain_out):
+    cells = gain_out.shape[0]
+    point_out[...] = moved[...].astype(F32)
+
+    @pl.when((pl.program_id(0) == 0) & (pl.program_id(1) == 0))
+    def _():
+        for j in range(cells):
+            depth_out[j, 0:8, :] = small[j]
+            depth_out[j, 8:9, :] = small[cells, j : j + 1, :]
+        gain_out[...] = small[cells, cells : 2 * cells, :]
 
 
 def local(images, cotangent, counts, gains, depthwise, pointwise):
     cells, channels = gains.shape
     sections = lax.axis_size("section")
-    slots = sections * cells
     replicas = lax.axis_size("dp")
     bits = replicas.bit_length() - 1
     assert sections == 2 and replicas == 1 << bits and cells == 4
@@ -444,21 +524,13 @@
 
     img = images.reshape(2, rows, channels)
     cot = cotangent.reshape(2, rows, channels)
-    active = (jnp.arange(cells) < counts[0]).astype(F32)[:, None, None]
-    pack = jnp.concatenate(
-        [
-            depthwise,
-            gains[:, None, :],
-            jnp.broadcast_to(active, (cells, 1, channels)),
-            jnp.zeros((cells, 5, channels), F32),
-        ],
-        axis=1,
-    )
+    used, masked = (cells, cells), True
+    slots = sum(used)
     landing = [
         pltpu.VMEM((slots, half >> min(b + 1, halvings), channels), BF16) for b in range(bits)
     ]
     steps = 2 + bits + halvings
-    plan = (cells, slots, bits, halvings, height, image_rows, per_core)
+    plan = (cells, used, masked, bits, halvings, height, image_rows, per_core)
     grid_rows = (cells + 1, 8, channels)
     moved, small = pl.pallas_call(
         functools.partial(kernel, plan),
@@ -466,13 +538,16 @@
             jax.ShapeDtypeStruct((cells, channels, channels), BF16),
             jax.ShapeDtypeStruct(grid_rows, F32),
         ),
-        in_specs=[pl.BlockSpec(memory_space=pl.ANY)] * 4,
+        in_specs=[pl.BlockSpec(memory_space=pl.ANY)] * 2
+        + [pl.BlockSpec(memory_space=pltpu.SMEM), pl.BlockSpec(memory_space=pltpu.VMEM)]
+        + [pl.BlockSpec(memory_space=pl.ANY)] * 2,
         out_specs=(
             pl.BlockSpec(memory_space=pltpu.VMEM),
             pl.BlockSpec(memory_space=pltpu.VMEM),
         ),
         scratch_shapes=[
-            pltpu.VMEM((slots, 16, channels), F32),
+            pltpu.VMEM((2 * cells, 9, channels), F32),
+            pltpu.VMEM((2, 2 * cells, channels), F32),
             pltpu.VMEM((slots, channels, channels), BF16),
             pltpu.VMEM((slots + 1, rows, channels), BF16),
             pltpu.VMEM((slots, rows, LANES), F32),
@@ -481,7 +556,7 @@
             pltpu.VMEM((slots, rows, channels), BF16),
             pltpu.VMEM((rows, channels), BF16),
             pltpu.VMEM((rows, channels), F32),
-            pltpu.VMEM((9, 8, channels), F32),
+            pltpu.VMEM((11, 8, channels), F32),
             pltpu.VMEM((9, 8, channels), F32),
             pltpu.VMEM((8, channels), F32),
             pltpu.VMEM((slots, channels, channels), BF16),
@@ -496,15 +571,26 @@
             pltpu.SemaphoreType.DMA((bits + 1,)),
             pltpu.SemaphoreType.DMA((cells,)),
             pltpu.SemaphoreType.DMA((slots,)),
-            pltpu.SemaphoreType.DMA((5,)),
+            pltpu.SemaphoreType.DMA((7,)),
         ]
         + landing,
         compiler_params=pltpu.CompilerParams(
-            collective_id=0, has_side_effects=True, vmem_limit_bytes=56 * 1024 * 1024
+            collective_id=0, has_side_effects=True, vmem_limit_bytes=48 * 1024 * 1024
         ),
-    )(img, cot, pack, pointwise)
-    depth = jnp.concatenate([small[:cells], small[cells, :cells][:, None, :]], axis=1)
-    return (moved.astype(F32), depth, small[cells, cells:])
+    )(img, cot, counts, gains, depthwise, pointwise)
+    whole = pl.BlockSpec(memory_space=pltpu.VMEM)
+    block = pl.BlockSpec((1, half, channels), lambda j, i: (j, i, 0))
+    return pl.pallas_call(
+        widen,
+        grid=(cells, 2),
+        out_shape=(
+            jax.ShapeDtypeStruct(pointwise.shape, F32),
+            jax.ShapeDtypeStruct(depthwise.shape, F32),
+            jax.ShapeDtypeStruct(gains.shape, F32),
+        ),
+        in_specs=[block, whole],
+        out_specs=(block, whole, whole),
+    )(moved, small)
 
 
 def solution(mesh):

time: 96.5 us -> 116 us (1.20)
  Pallas kernels: 85.2 us -> 106 us
  other arithmetic: 4.94 us -> 0 us
  local copies, waits for them, and re-layouts: 4.7 us -> 8.83 us
    pallas_call x1, Pallas kernels: 85.2 us -> 99.5 us  [local(): pl.pallas_call(functools.partial(kernel, plan), out_shape=(jax.ShapeDtype...]
    pallas_call x0 -> x1, Pallas kernels: none -> 6.06 us  [local(): pl.pallas_call(widen, grid=(cells, 2), out_shape=(jax.ShapeDtypeStruct(po...]
    unnamed x2 -> x13, local copies, waits for them, and re-layouts: 1.59 us -> 7.24 us
    convert_element_type x2 -> x0, other arithmetic: 4.2 us -> none  [the longest x1 4.19 us: local(): return (moved.astype(F32), depth, small[cells, cells:])]
    pallas_call x0 -> x1, local copies, waits for them, and re-layouts: none -> 1.59 us  [local(): pl.pallas_call(widen, grid=(cells, 2), out_shape=(jax.ShapeDtypeStruct(po...]
    squeeze x1 -> x0, local copies, waits for them, and re-layouts: 1.4 us -> none  [local(): return (moved.astype(F32), depth, small[cells, cells:])]
where the time goes in v1:
time: 116 us
  Pallas kernels  106 us (91%)
  local copies, waits for them, and re-layouts  8.83 us (8%)
  between operations  1.31 us (1%)
    pallas_call x1, Pallas kernels, local(): pl.pallas_call(functools.partial(kernel, plan), out_shape=(jax.ShapeDtype...  99.5 us
    unnamed x13, local copies, waits for them, and re-layouts  7.24 us
    pallas_call x1, Pallas kernels, local(): pl.pallas_call(widen, grid=(cells, 2), out_shape=(jax.ShapeDtypeStruct(po...  6.06 us

profile of v1, /device:TPU:0, one launch (start us, length us, event | category | flops | bytes accessed | tf_op | source)
XLA Modules:
  0.0 115.7 jit_solution(13043972057547577579)
XLA Ops:
  1.3 0.9 copy.9.depth_in
  2.2 0.0 copy-start
  2.2 1.6 %copy-done = bf16[4,512,512]{2,1,0:T(8,128)(2,1)S(1)} copy-done((bf16[4,512,512]{2,1,0:T(8,128)(2,1)S(1)}, bf16[4,512,512]{2,1,0:T(8,128)(2,1)}, u32[]{:S(2)}) %copy-start) | copy-done | bytes 2097176
  3.8 0.0 copy-start.2
  3.8 1.0 copy-done.2
  4.8 0.0 copy-start.3
  4.8 1.0 copy-done.3
  5.9 0.0 copy-start.5
  5.9 0.7 copy-done.5
  6.6 99.5 %shard_map.85 = (bf16[4,512,512]{2,1,0:T(8,128)(2,1)S(1)}, f32[5,8,512]{2,1,0:T(8,128)S(1)}) custom-call(bf16[2,256,512]{2,1,0:T(8,128)(2,1)S(1)} %bitcast.2, bf16[2,256,512]{2,1,0:T(8,128)(2,1)S(1)} %bitcast.3, s32[1]{0:T(128)S(6)} %copy.11.counts, f32[4,512]{1,0:T(4,128)S(1)} %copy-done.5, f32[4,9,512]{2,1,0:T(8,128)S(1)} %copy.9.depth_in, ...), custom_call_target="tpu_custom_call" | custom-call | tf_op jit(solution)/shard_map/pallas_call | solution.py:535
  106.1 0.0 copy-start.1
  106.1 1.3 %copy-done.1 = bf16[4,512,512]{2,1,0:T(8,128)(2,1)} copy-done((bf16[4,512,512]{2,1,0:T(8,128)(2,1)}, bf16[4,512,512]{2,1,0:T(8,128)(2,1)S(1)}, u32[]{:S(2)}) %copy-start.1) | copy-done | bytes 2097176
  107.5 0.0 copy-start.4
  107.5 0.6 copy-done.4
  108.1 6.1 %shard_map.86 = (f32[4,512,512]{2,1,0:T(8,128)}, f32[4,9,512]{2,1,0:T(8,128)}, f32[4,512]{1,0:T(4,128)}) custom-call(bf16[4,512,512]{2,1,0:T(8,128)(2,1)} %copy-done.1, f32[5,8,512]{2,1,0:T(8,128)} %copy-done.4), custom_call_target="tpu_custom_call" | custom-call | tf_op jit(solution)/shard_map/pallas_call | solution.py:583
  114.1 1.6 %copy.10 = f32[4,9,512]{2,0,1:T(4,128)} copy(f32[4,9,512]{2,1,0:T(8,128)} %get-tuple-element.8) | data formatting | bytes 147456 | tf_op jit(solution)/shard_map/pallas_call | solution.py:583
Async XLA Ops:
  2.2 1.6 %copy-start = (bf16[4,512,512]{2,1,0:T(8,128)(2,1)S(1)}, bf16[4,512,512]{2,1,0:T(8,128)(2,1)}, u32[]{:S(2)}) copy-start(bf16[4,512,512]{2,1,0:T(8,128)(2,1)} %point_in.1) | copy-start | bytes 6291460
  3.8 1.0 copy-start.2
  4.8 1.0 copy-start.3
  5.9 0.7 copy-start.5
  106.1 1.3 %copy-start.1 = (bf16[4,512,512]{2,1,0:T(8,128)(2,1)}, bf16[4,512,512]{2,1,0:T(8,128)(2,1)S(1)}, u32[]{:S(2)}) copy-start(bf16[4,512,512]{2,1,0:T(8,128)(2,1)S(1)} %get-tuple-element.5.moved) | copy-start | bytes 6291460
  107.5 0.6 copy-start.4

commit v2 on v1

--- a/solution.py
+++ b/solution.py
@@ -13,6 +13,7 @@
 TILE = 16
 F32 = jnp.float32
 BF16 = jnp.bfloat16
+PIECES = 4
 
 
 def kernel(
@@ -24,7 +25,8 @@
     depth_in,
     point_in,
     out,
-    small_out,
+    depth_out,
+    gain_out,
     depth,
     meta,
     point,
@@ -53,8 +55,9 @@
     load_sem,
     *landing,
 ):
-    cells, used, masked, bits, halvings, height, image_rows, images = plan
+    cells, used, masked, bits, height, image_rows, images = plan
     slots = sum(used)
+    doublings = bits - 4
     rows = images * image_rows
     channels = point.shape[-1]
     half = channels // 2
@@ -80,13 +83,16 @@
 
     barrier = pltpu.get_barrier_semaphore()
     pl.semaphore_signal(barrier, inc=1, device_id=(sibling, me), device_id_type=MESH)
-    for partner in partners:
+    ring = lax.rem(me // 4, 4)
+    peers = [lax.rem(ring + r, 4) for r in range(4)]
+    ring_partners = [me + (peer - ring) * 4 for peer in peers]
+    for partner in partners[:2] + ring_partners[1:] + partners[4:]:
         pl.semaphore_signal(barrier, inc=1, device_id=(core, partner), device_id_type=MESH)
 
     load_img = pltpu.make_async_copy(img.at[core], xs.at[0], load_sem.at[0])
     load_cot = pltpu.make_async_copy(cot.at[core], gy, load_sem.at[1])
     load_depth = pltpu.make_async_copy(
-        depth_in, depth.at[pl.ds(core * cells, cells)], load_sem.at[2]
+        depth_in, depth.at[core], load_sem.at[2]
     )
     load_img.start()
     load_depth.start()
@@ -116,7 +122,7 @@
         meta[core, cells + j : cells + j + 1, :] = jnp.where(
             jnp.full((1, channels), j, jnp.int32) < counts[0], 1.0, 0.0
         )
-    pl.semaphore_wait(barrier, 1 + bits)
+    pl.semaphore_wait(barrier, 2 + bits)
 
     def to_sibling(src, dst, send, recv):
         return pltpu.make_async_remote_copy(
@@ -130,20 +136,27 @@
 
     def depth_copy():
         return to_sibling(
-            depth_in, depth.at[pl.ds(core * cells, cells)], load_sem.at[3], load_sem.at[4]
+            depth_in, depth.at[core], load_sem.at[3], load_sem.at[4]
         )
 
     def meta_copy():
         return to_sibling(meta.at[core], meta.at[core], load_sem.at[5], load_sem.at[6])
 
-    def point_copy(j):
+    def point_copy(j, part=slice(None)):
         return to_sibling(
-            point_in.at[j], point.at[place(j)], weight_send.at[j], weight_recv.at[place(j)]
-        )
+            point_in.at[j, part],
+            point.at[place(j), part],
+            weight_send.at[j],
+            weight_recv.at[place(j)],
+        )
+
+    def point_send(j):
+        for piece in range(PIECES):
+            point_copy(j, pl.ds(piece * (channels // PIECES), channels // PIECES)).start()
 
     depth_copy().start()
     meta_copy().start()
-    each_cell(lambda j: point_copy(j).start())
+    each_cell(point_send)
     load_img.wait()
     load_depth.wait()
     depth_copy().wait()
@@ -157,7 +170,7 @@
             for q in range(3):
                 t = p * 3 + q
                 tile = jnp.broadcast_to(
-                    depth[segment * cells + j, t : t + 1, :], (8, channels)
+                    depth[segment, t, pl.ds(j, 1), :], (8, channels)
                 )
                 if q == 0:
                     tile = jnp.where(column == low_tap_edge, 0.0, tile)
@@ -210,7 +223,7 @@
                 slope_all[k, at, lane(b)] = sigma + act * (1.0 - sigma)
             return carry
 
-        lax.fori_loop(0, images, image, 0)
+        lax.fori_loop(0, images, image, 0, unroll=2)
         mixed = jnp.dot(act_all[k], point[k], preferred_element_type=F32)
         x = xs[k].astype(F32)
         y = x + mixed
@@ -238,44 +251,94 @@
 
     keep, away, sizes = [], [], []
     offset, size = base, half
-    for b in range(bits):
-        if b < halvings:
-            size = size // 2
-            away.append(offset + (1 - digits[b]) * size)
-            offset = offset + digits[b] * size
-        else:
-            away.append(offset)
+    for b in range(2):
+        size = size // 2
+        away.append(offset + (1 - digits[b]) * size)
+        offset = offset + digits[b] * size
         keep.append(offset)
         sizes.append(size)
-
-    def core_copy(k):
+    size = size // 4
+    own = offset + ring * size
+
+    def pieces(make, start, size, count):
+        for piece in range(count):
+            make(start + piece * (size // count), size // count).start()
+
+    def core_copy(k, start, size):
         return remote(
-            grads.at[k, span(sibling * half, half)], from_core.at[k], k, 0, (sibling, me)
-        )
-
-    def scatter_copy(k, b):
+            grads.at[k, span(sibling * half + start, size)],
+            from_core.at[k, span(start, size)],
+            k,
+            0,
+            (sibling, me),
+        )
+
+    def pair_copy(k, b, start, size):
         return remote(
-            grads.at[k, span(away[b], sizes[b])], landing[b].at[k], k, 1 + b, (core, partners[b])
-        )
-
-    def gather_copy(k, b):
-        part = span(keep[b], sizes[b])
+            grads.at[k, span(away[b] + start, size)],
+            landing[b].at[k, span(start, size)],
+            k,
+            1 + b,
+            (core, partners[b]),
+        )
+
+    def send_pair(k, b):
+        pieces(lambda start, size: pair_copy(k, b, start, size), 0, sizes[b], 2)
+
+    def ring_copy(k, r):
         return remote(
-            reduced.at[k, part], reduced.at[k, part], k, 1 + bits + b, (core, partners[b])
-        )
-
-    def home_copy(k):
-        part = span(base, half)
+            grads.at[k, span(offset + peers[r] * size, size)],
+            landing[2].at[k, r - 1],
+            k,
+            2 + r,
+            (core, ring_partners[r]),
+        )
+
+    def double_copy(k, d):
+        return remote(
+            grads.at[k, span(own, size)], landing[3 + d].at[k], k, 9 + d, (core, partners[4 + d])
+        )
+
+    def spread_copy(k, r):
+        part = span(own, size)
+        return remote(
+            reduced.at[k, part],
+            reduced.at[k, part],
+            k,
+            5 + r,
+            (core, ring_partners[r]),
+        )
+
+    def gather_copy(k, b, start, size):
+        part = span(keep[b] + start, size)
+        return remote(
+            reduced.at[k, part], reduced.at[k, part], k, 9 + doublings + b, (core, partners[b])
+        )
+
+    def send_gather(k, b):
+        pieces(lambda start, size: gather_copy(k, b, start, size), 0, sizes[b], 2)
+
+    def home_copy(k, start, size):
+        part = span(base + start, size)
         return remote(
             reduced.at[k, part],
             out.at[owner(k)[1], part],
             k,
-            1 + bits + halvings,
+            11 + doublings,
             (sibling, me),
         )
 
-    def add_landed(k, part, landed):
-        grads[k, part] = (grads[k, part].astype(F32) + landed.astype(F32)).astype(BF16)
+    def add_landed(k, part, *landed):
+        total = grads[k, part].astype(F32)
+        for block in landed:
+            total = total + block.astype(F32)
+        grads[k, part] = total.astype(BF16)
+
+    def spread(k):
+        part = span(own, size)
+        reduced[k, part] = grads[k, part]
+        for r in range(1, 4):
+            spread_copy(k, r).start()
 
     def finish(k):
         part = span(base, half)
@@ -283,46 +346,59 @@
 
         @pl.when(core != segment)
         def _():
-            home_copy(k).start()
+            pieces(lambda start, size: home_copy(k, start, size), 0, half, PIECES)
 
         @pl.when(core == segment)
         def _():
             out[j, part] = reduced[k, part]
 
+    last_age = 7 + doublings
+
     def stage(k, age):
-        if age <= bits:
-            b = age - 1
-            scatter_copy(k, b).wait()
+        if age == 1:
+            core_copy(k, 0, half).wait()
+            add_landed(k, span(base, half), from_core[k])
+            send_pair(k, 0)
+        elif age <= 3:
+            b = age - 2
+            pair_copy(k, b, 0, sizes[b]).wait()
             add_landed(k, span(keep[b], sizes[b]), landing[b][k])
-            if age < bits:
-                scatter_copy(k, age).start()
+            if b == 0:
+                send_pair(k, 1)
             else:
-                part = span(offset, size)
-                reduced[k, part] = grads[k, part]
-                gather_copy(k, halvings - 1).start()
+                for r in range(1, 4):
+                    ring_copy(k, r).start()
+        elif age <= 4 + doublings:
+            d = age - 4
+            if d == 0:
+                for r in range(1, 4):
+                    ring_copy(k, r).wait()
+                add_landed(k, span(own, size), *[landing[2][k, r] for r in range(3)])
+            else:
+                double_copy(k, d - 1).wait()
+                add_landed(k, span(own, size), landing[2 + d][k])
+            if d < doublings:
+                double_copy(k, d).start()
+            else:
+                spread(k)
+        elif age == 5 + doublings:
+            for r in range(1, 4):
+                spread_copy(k, r).wait()
+            send_gather(k, 1)
+        elif age == 6 + doublings:
+            gather_copy(k, 1, 0, sizes[1]).wait()
+            send_gather(k, 0)
         else:
-            b = halvings - (age - bits)
-            gather_copy(k, b).wait()
-            if b > 0:
-                gather_copy(k, b - 1).start()
-            else:
-                finish(k)
-
-    last_age = bits + halvings
-
-    def pump(n, middle):
-        ages = [a for a in range(1, last_age + 1) if a % 2 == (1 if middle else 0)]
-        ages.sort(key=lambda a: sizes_of[a])
-        for age in ages:
-            turn = (age + 1) // 2 if middle else 1 + age // 2
-
-            @pl.when((n >= turn) & (n < turn + slots))
-            def _(age=age, turn=turn):
-                stage(slots - 1 - (n - turn), age)
-
-    sizes_of = {}
-    for a in range(1, last_age + 1):
-        sizes_of[a] = sizes[a - 1] if a <= bits else sizes[halvings - (a - bits)]
+            gather_copy(k, 0, 0, sizes[0]).wait()
+            finish(k)
+
+    def pump(n):
+        order = list(range(4, 6 + doublings)) + [3, 6 + doublings, 2, 7 + doublings, 1]
+        for age in order:
+
+            @pl.when((n >= age) & (n < age + slots))
+            def _(age=age):
+                stage(slots - 1 - (n - age), age)
 
     def small_copy(step):
         if step == 0:
@@ -346,7 +422,11 @@
             small_sum[age - 1] = total
             small_copy(age).start()
         else:
-            small_out[...] = total
+            for j in range(cells):
+                for t in range(8):
+                    depth_out[t, j : j + 1, :] = total[j, t : t + 1, :]
+            depth_out[8] = total[cells, :cells]
+            gain_out[...] = total[cells, cells:]
 
     small[...] = jnp.zeros_like(small)
     for j in range(cells):
@@ -365,14 +445,13 @@
         if masked:
             gp = jnp.where(stacked(taps[10], channels) > 0.5, gp, 0.0)
         grads[k] = gp.astype(BF16)
-        core_copy(k).start()
+        pieces(lambda start, size: core_copy(k, start, size), 0, half, PIECES)
         ga = lax.dot_general(
             gy[...], point[k], (((1,), (1,)), ((), ())), preferred_element_type=F32
         )
         gl[...] = ga * slope_all[k]
         tap_acc[...] = jnp.zeros_like(tap_acc)
         gain_acc[...] = jnp.zeros_like(gain_acc)
-        pump(n, True)
 
         def image(i, carry):
             at = pl.ds(pl.multiple_of(i * image_rows, image_rows), image_rows)
@@ -428,10 +507,7 @@
                 gy[at, lane(b)] = gx.astype(BF16)
             return carry
 
-        lax.fori_loop(0, images, image, 0)
-        core_copy(k).wait()
-        add_landed(k, span(base, half), from_core[k])
-        scatter_copy(k, 0).start()
+        lax.fori_loop(0, images, image, 0, unroll=2)
 
         segment, j = owner(k)
         on = taps[10, 0:1, :] > 0.5
@@ -453,29 +529,25 @@
         small[segment, cells, pl.ds(cells + j, 1), :] = gain
 
     def turn(n, carry):
-        pump(n, False)
+        pump(n)
 
         @pl.when(n < slots)
         def _():
             backward(n)
 
-        @pl.when(n >= slots)
-        def _():
-            pump(n, True)
-
         @pl.when(n == slots - 1)
         def _():
             small_copy(0).start()
 
         for age in range(1, bits + 2):
 
-            @pl.when(n == slots + (age - 1) // 2)
+            @pl.when(n == slots - 1 + age)
             def _(age=age):
                 small_stage(age)
 
         return carry
 
-    lax.fori_loop(0, slots + 1 + max(last_age // 2, (bits + 2) // 2), turn, 0)
+    lax.fori_loop(0, slots + max(last_age, bits + 1), turn, 0)
 
     def wait_home(n, carry):
         k = slots - 1 - n
@@ -483,27 +555,15 @@
 
         @pl.when(core != segment)
         def _():
-            home_copy(k).wait_send()
+            home_copy(k, 0, half).wait_send()
 
         @pl.when(core == segment)
         def _():
-            home_copy(k).wait_recv()
+            home_copy(k, 0, half).wait_recv()
 
         return carry
 
     lax.fori_loop(0, slots, wait_home, 0)
-
-
-def widen(moved, small, point_out, depth_out, gain_out):
-    cells = gain_out.shape[0]
-    point_out[...] = moved[...].astype(F32)
-
-    @pl.when((pl.program_id(0) == 0) & (pl.program_id(1) == 0))
-    def _():
-        for j in range(cells):
-            depth_out[j, 0:8, :] = small[j]
-            depth_out[j, 8:9, :] = small[cells, j : j + 1, :]
-        gain_out[...] = small[cells, cells : 2 * cells, :]
 
 
 def local(images, cotangent, counts, gains, depthwise, pointwise):
@@ -518,35 +578,34 @@
     per_core = micro * batch // 2
     rows = per_core * image_rows
     half = channels // 2
-    halvings = 0
-    while halvings < bits and (half >> (halvings + 1)) % TILE == 0 and (half >> (halvings + 1)):
-        halvings += 1
+    assert bits >= 4 and half % (16 * TILE) == 0
 
     img = images.reshape(2, rows, channels)
     cot = cotangent.reshape(2, rows, channels)
     used, masked = (cells, cells), True
     slots = sum(used)
+    piece = half // 16
     landing = [
-        pltpu.VMEM((slots, half >> min(b + 1, halvings), channels), BF16) for b in range(bits)
-    ]
-    steps = 2 + bits + halvings
-    plan = (cells, used, masked, bits, halvings, height, image_rows, per_core)
+        pltpu.VMEM((slots, half // 2, channels), BF16),
+        pltpu.VMEM((slots, half // 4, channels), BF16),
+        pltpu.VMEM((slots, 3, piece, channels), BF16),
+    ] + [pltpu.VMEM((slots, piece, channels), BF16)] * (bits - 4)
+    steps = 8 + bits
+    plan = (cells, used, masked, bits, height, image_rows, per_core)
     grid_rows = (cells + 1, 8, channels)
-    moved, small = pl.pallas_call(
+    point, depth, gain = pl.pallas_call(
         functools.partial(kernel, plan),
         out_shape=(
             jax.ShapeDtypeStruct((cells, channels, channels), BF16),
-            jax.ShapeDtypeStruct(grid_rows, F32),
+            jax.ShapeDtypeStruct((9, cells, channels), F32),
+            jax.ShapeDtypeStruct((cells, channels), F32),
         ),
         in_specs=[pl.BlockSpec(memory_space=pl.ANY)] * 2
         + [pl.BlockSpec(memory_space=pltpu.SMEM), pl.BlockSpec(memory_space=pltpu.VMEM)]
         + [pl.BlockSpec(memory_space=pl.ANY)] * 2,
-        out_specs=(
-            pl.BlockSpec(memory_space=pltpu.VMEM),
-            pl.BlockSpec(memory_space=pltpu.VMEM),
-        ),
+        out_specs=(pl.BlockSpec(memory_space=pltpu.VMEM),) * 3,
         scratch_shapes=[
-            pltpu.VMEM((2 * cells, 9, channels), F32),
+            pltpu.VMEM((2, 9, cells, channels), F32),
             pltpu.VMEM((2, 2 * cells, channels), F32),
             pltpu.VMEM((slots, channels, channels), BF16),
             pltpu.VMEM((slots + 1, rows, channels), BF16),
@@ -575,22 +634,10 @@
         ]
         + landing,
         compiler_params=pltpu.CompilerParams(
-            collective_id=0, has_side_effects=True, vmem_limit_bytes=48 * 1024 * 1024
+            collective_id=0, has_side_effects=True, vmem_limit_bytes=60 * 1024 * 1024
         ),
-    )(img, cot, counts, gains, depthwise, pointwise)
-    whole = pl.BlockSpec(memory_space=pltpu.VMEM)
-    block = pl.BlockSpec((1, half, channels), lambda j, i: (j, i, 0))
-    return pl.pallas_call(
-        widen,
-        grid=(cells, 2),
-        out_shape=(
-            jax.ShapeDtypeStruct(pointwise.shape, F32),
-            jax.ShapeDtypeStruct(depthwise.shape, F32),
-            jax.ShapeDtypeStruct(gains.shape, F32),
-        ),
-        in_specs=[block, whole],
-        out_specs=(block, whole, whole),
-    )(moved, small)
+    )(img, cot, counts, gains, depthwise.transpose(1, 0, 2), pointwise)
+    return (point.astype(F32), depth.transpose(1, 0, 2), gain)
 
 
 def solution(mesh):

time: 116 us -> 86.3 us (0.74)
  Pallas kernels: 106 us -> 79.3 us
  local copies, waits for them, and re-layouts: 8.83 us -> 1.24 us
  other arithmetic: 0 us -> 4.22 us
    pallas_call x1, Pallas kernels: 99.5 us -> 79.3 us  [local(): pl.pallas_call(functools.partial(kernel, plan), out_shape=(jax.ShapeDtype...]
    pallas_call x1 -> x0, Pallas kernels: 6.06 us -> none  [local(): pl.pallas_call(widen, grid=(cells, 2), out_shape=(jax.ShapeDtypeStruct(po...]
    unnamed x13 -> x6, local copies, waits for them, and re-layouts: 7.24 us -> 1.24 us
    convert_element_type x0 -> x1, other arithmetic: none -> 4.22 us  [local(): return (point.astype(F32), depth.transpose(1, 0, 2), gain)]
    pallas_call x1 -> x0, local copies, waits for them, and re-layouts: 1.59 us -> none  [local(): pl.pallas_call(widen, grid=(cells, 2), out_shape=(jax.ShapeDtypeStruct(po...]
where the time goes in v2:
time: 86.3 us; the launch traced here: 86.1 us
  Pallas kernels  79.3 us (92%)
  other arithmetic  4.22 us (5%)
  between operations  1.3 us (2%)
  local copies, waits for them, and re-layouts  1.24 us (1%)
    pallas_call x1, Pallas kernels, local(): pl.pallas_call(functools.partial(kernel, plan), out_shape=(jax.ShapeDtype...  79.3 us
    convert_element_type x1, other arithmetic, local(): return (point.astype(F32), depth.transpose(1, 0, 2), gain)  4.22 us

profile of v2, /device:TPU:0, one launch (start us, length us, event | category | flops | bytes accessed | tf_op | source)
XLA Modules:
  0.0 86.1 jit_solution(5868778228470788203)
XLA Ops:
  1.3 79.3 %shard_map.85 = (bf16[4,512,512]{2,1,0:T(8,128)(2,1)}, f32[9,4,512]{2,1,0:T(4,128)}, f32[4,512]{1,0:T(4,128)}) custom-call(bf16[2,256,512]{2,1,0:T(8,128)(2,1)} %bitcast.4, bf16[2,256,512]{2,1,0:T(8,128)(2,1)} %bitcast.5, s32[1]{0:T(128)S(6)} %copy.11.counts, f32[4,512]{1,0:T(4,128)} %gains.1, f32[9,4,512]{2,1,0:T(4,128)} %bitcast.6, ...), custom_call_target="tpu_custom_call" | custom-call | tf_op jit(solution)/shard_map/pallas_call | solution.py:596
  80.6 0.0 copy-start
  80.6 0.0 copy-start.1
  80.6 4.2 %convert_element_type.3 = f32[4,512,512]{2,1,0:T(8,128)} convert(bf16[4,512,512]{2,1,0:T(8,128)(2,1)} %get-tuple-element.6) | non-fusion elementwise | flops 1048576 | bytes 6291456 | tf_op jit(solution)/shard_map/convert_element_type | solution.py:640
  84.9 0.0 copy-done
  84.9 0.6 copy.12
  85.5 0.0 copy-done.1
  85.5 0.6 copy.13
Async XLA Ops:
  80.6 4.2 %copy-start = (f32[9,4,512]{2,1,0:T(4,128)S(1)}, f32[9,4,512]{2,1,0:T(4,128)}, u32[]{:S(2)}) copy-start(f32[9,4,512]{2,1,0:T(4,128)} %get-tuple-element.7) | copy-start | bytes 221188
  80.6 4.9 %copy-start.1 = (f32[4,512]{1,0:T(4,128)S(1)}, f32[4,512]{1,0:T(4,128)}, u32[]{:S(2)}) copy-start(f32[4,512]{1,0:T(4,128)} %get-tuple-element.14) | copy-start | bytes 24580

commit v3 on v2

--- a/solution.py
+++ b/solution.py
@@ -82,7 +82,8 @@
     base = core * half
 
     barrier = pltpu.get_barrier_semaphore()
-    pl.semaphore_signal(barrier, inc=1, device_id=(sibling, me), device_id_type=MESH)
+    for home in (me, partners[1]):
+        pl.semaphore_signal(barrier, inc=1, device_id=(sibling, home), device_id_type=MESH)
     ring = lax.rem(me // 4, 4)
     peers = [lax.rem(ring + r, 4) for r in range(4)]
     ring_partners = [me + (peer - ring) * 4 for peer in peers]
@@ -122,7 +123,7 @@
         meta[core, cells + j : cells + j + 1, :] = jnp.where(
             jnp.full((1, channels), j, jnp.int32) < counts[0], 1.0, 0.0
         )
-    pl.semaphore_wait(barrier, 2 + bits)
+    pl.semaphore_wait(barrier, 3 + bits)
 
     def to_sibling(src, dst, send, recv):
         return pltpu.make_async_remote_copy(
@@ -318,14 +319,16 @@
     def send_gather(k, b):
         pieces(lambda start, size: gather_copy(k, b, start, size), 0, sizes[b], 2)
 
-    def home_copy(k, start, size):
-        part = span(base + start, size)
+    homes = (me, partners[0])
+
+    def home_copy(k, to, start, size):
+        part = span(keep[0] + start, size)
         return remote(
             reduced.at[k, part],
             out.at[owner(k)[1], part],
             k,
-            11 + doublings,
-            (sibling, me),
+            11 + doublings + to,
+            (sibling, homes[to]),
         )
 
     def add_landed(k, part, *landed):
@@ -340,17 +343,27 @@
         for r in range(1, 4):
             spread_copy(k, r).start()
 
+    def owned(k):
+        return core == owner(k)[0]
+
+    def send_home(k):
+        @pl.when(owned(k))
+        def _():
+            send_gather(k, 0)
+
+        @pl.when(core != owner(k)[0])
+        def _():
+            for to in (1, 0):
+                pieces(
+                    lambda start, size: home_copy(k, to, start, size), 0, sizes[0], PIECES // 2
+                )
+
     def finish(k):
-        part = span(base, half)
-        segment, j = owner(k)
-
-        @pl.when(core != segment)
+        @pl.when(owned(k))
         def _():
-            pieces(lambda start, size: home_copy(k, start, size), 0, half, PIECES)
-
-        @pl.when(core == segment)
-        def _():
-            out[j, part] = reduced[k, part]
+            part = span(base, half)
+            gather_copy(k, 0, 0, sizes[0]).wait()
+            out[owner(k)[1], part] = reduced[k, part]
 
     last_age = 7 + doublings
 
@@ -387,9 +400,8 @@
             send_gather(k, 1)
         elif age == 6 + doublings:
             gather_copy(k, 1, 0, sizes[1]).wait()
-            send_gather(k, 0)
+            send_home(k)
         else:
-            gather_copy(k, 0, 0, sizes[0]).wait()
             finish(k)
 
     def pump(n):
@@ -551,15 +563,15 @@
 
     def wait_home(n, carry):
         k = slots - 1 - n
-        segment, _ = owner(k)
-
-        @pl.when(core != segment)
-        def _():
-            home_copy(k, 0, half).wait_send()
-
-        @pl.when(core == segment)
-        def _():
-            home_copy(k, 0, half).wait_recv()
+        for to in (0, 1):
+
+            @pl.when(core != owner(k)[0])
+            def _(to=to):
+                home_copy(k, to, 0, sizes[0]).wait_send()
+
+            @pl.when(owned(k))
+            def _(to=to):
+                home_copy(k, to, 0, sizes[0]).wait_recv()
 
         return carry
 
@@ -582,62 +594,82 @@
 
     img = images.reshape(2, rows, channels)
     cot = cotangent.reshape(2, rows, channels)
-    used, masked = (cells, cells), True
-    slots = sum(used)
-    piece = half // 16
-    landing = [
-        pltpu.VMEM((slots, half // 2, channels), BF16),
-        pltpu.VMEM((slots, half // 4, channels), BF16),
-        pltpu.VMEM((slots, 3, piece, channels), BF16),
-    ] + [pltpu.VMEM((slots, piece, channels), BF16)] * (bits - 4)
-    steps = 8 + bits
-    plan = (cells, used, masked, bits, height, image_rows, per_core)
-    grid_rows = (cells + 1, 8, channels)
-    point, depth, gain = pl.pallas_call(
-        functools.partial(kernel, plan),
-        out_shape=(
-            jax.ShapeDtypeStruct((cells, channels, channels), BF16),
-            jax.ShapeDtypeStruct((9, cells, channels), F32),
-            jax.ShapeDtypeStruct((cells, channels), F32),
-        ),
-        in_specs=[pl.BlockSpec(memory_space=pl.ANY)] * 2
-        + [pl.BlockSpec(memory_space=pltpu.SMEM), pl.BlockSpec(memory_space=pltpu.VMEM)]
-        + [pl.BlockSpec(memory_space=pl.ANY)] * 2,
-        out_specs=(pl.BlockSpec(memory_space=pltpu.VMEM),) * 3,
-        scratch_shapes=[
-            pltpu.VMEM((2, 9, cells, channels), F32),
-            pltpu.VMEM((2, 2 * cells, channels), F32),
-            pltpu.VMEM((slots, channels, channels), BF16),
-            pltpu.VMEM((slots + 1, rows, channels), BF16),
-            pltpu.VMEM((slots, rows, LANES), F32),
-            pltpu.VMEM((slots, rows, channels), F32),
-            pltpu.VMEM((slots, rows, channels), F32),
-            pltpu.VMEM((slots, rows, channels), BF16),
-            pltpu.VMEM((rows, channels), BF16),
-            pltpu.VMEM((rows, channels), F32),
-            pltpu.VMEM((11, 8, channels), F32),
-            pltpu.VMEM((9, 8, channels), F32),
-            pltpu.VMEM((8, channels), F32),
-            pltpu.VMEM((slots, channels, channels), BF16),
-            pltpu.VMEM((slots, channels, channels), BF16),
-            pltpu.VMEM((slots, half, channels), BF16),
-            pltpu.VMEM((2,) + grid_rows, F32),
-            pltpu.VMEM((bits + 1,) + grid_rows, F32),
-            pltpu.VMEM((max(bits, 1),) + grid_rows, F32),
-            pltpu.SemaphoreType.DMA((slots, steps)),
-            pltpu.SemaphoreType.DMA((slots, steps)),
-            pltpu.SemaphoreType.DMA((bits + 1,)),
-            pltpu.SemaphoreType.DMA((bits + 1,)),
-            pltpu.SemaphoreType.DMA((cells,)),
-            pltpu.SemaphoreType.DMA((slots,)),
-            pltpu.SemaphoreType.DMA((7,)),
-        ]
-        + landing,
-        compiler_params=pltpu.CompilerParams(
-            collective_id=0, has_side_effects=True, vmem_limit_bytes=60 * 1024 * 1024
-        ),
-    )(img, cot, counts, gains, depthwise.transpose(1, 0, 2), pointwise)
-    return (point.astype(F32), depth.transpose(1, 0, 2), gain)
+    choices = [(cells, cells - i) for i in range(cells)]
+    choices += [(cells - i, cells) for i in range(1, cells)]
+
+    def run(number, counts, img, cot, gains, depthwise, pointwise):
+        used = choices[number]
+        slots = sum(used)
+        piece = half // 16
+        landing = [
+            pltpu.VMEM((slots, half // 2, channels), BF16),
+            pltpu.VMEM((slots, half // 4, channels), BF16),
+            pltpu.VMEM((slots, 3, piece, channels), BF16),
+        ] + [pltpu.VMEM((slots, piece, channels), BF16)] * (bits - 4)
+        steps = 9 + bits
+        plan = (cells, used, False, bits, height, image_rows, per_core)
+        grid_rows = (cells + 1, 8, channels)
+        point, depth, gain = pl.pallas_call(
+            functools.partial(kernel, plan),
+            out_shape=(
+                jax.ShapeDtypeStruct((cells, channels, channels), BF16),
+                jax.ShapeDtypeStruct((9, cells, channels), F32),
+                jax.ShapeDtypeStruct((cells, channels), F32),
+            ),
+            in_specs=[pl.BlockSpec(memory_space=pl.ANY)] * 2
+            + [pl.BlockSpec(memory_space=pltpu.SMEM), pl.BlockSpec(memory_space=pltpu.VMEM)]
+            + [pl.BlockSpec(memory_space=pl.ANY)] * 2,
+            out_specs=(pl.BlockSpec(memory_space=pltpu.VMEM),) * 3,
+            scratch_shapes=[
+                pltpu.VMEM((2, 9, cells, channels), F32),
+                pltpu.VMEM((2, 2 * cells, channels), F32),
+                pltpu.VMEM((slots, channels, channels), BF16),
+                pltpu.VMEM((slots + 1, rows, channels), BF16),
+                pltpu.VMEM((slots, rows, LANES), F32),
+                pltpu.VMEM((slots, rows, channels), F32),
+                pltpu.VMEM((slots, rows, channels), F32),
+                pltpu.VMEM((slots, rows, channels), BF16),
+                pltpu.VMEM((rows, channels), BF16),
+                pltpu.VMEM((rows, channels), F32),
+                pltpu.VMEM((11, 8, channels), F32),
+                pltpu.VMEM((9, 8, channels), F32),
+                pltpu.VMEM((8, channels), F32),
+                pltpu.VMEM((slots, channels, channels), BF16),
+                pltpu.VMEM((slots, channels, channels), BF16),
+                pltpu.VMEM((slots, half, channels), BF16),
+                pltpu.VMEM((2,) + grid_rows, F32),
+                pltpu.VMEM((bits + 1,) + grid_rows, F32),
+                pltpu.VMEM((max(bits, 1),) + grid_rows, F32),
+                pltpu.SemaphoreType.DMA((slots, steps)),
+                pltpu.SemaphoreType.DMA((slots, steps)),
+                pltpu.SemaphoreType.DMA((bits + 1,)),
+                pltpu.SemaphoreType.DMA((bits + 1,)),
+                pltpu.SemaphoreType.DMA((cells,)),
+                pltpu.SemaphoreType.DMA((slots,)),
+                pltpu.SemaphoreType.DMA((7,)),
+            ]
+            + landing,
+            compiler_params=pltpu.CompilerParams(
+                collective_id=number, has_side_effects=True, vmem_limit_bytes=60 * 1024 * 1024
+            ),
+        )(img, cot, counts, gains, depthwise.transpose(1, 0, 2), pointwise)
+        return (point.astype(F32), depth.transpose(1, 0, 2), gain)
+
+    other = lax.ppermute(counts, "section", [(0, 1), (1, 0)])
+    is_first = lax.axis_index("section") == 0
+    first = jnp.where(is_first, counts[0], other[0])
+    second = jnp.where(is_first, other[0], counts[0])
+    choice = jnp.where(first == cells, cells - second, 2 * cells - 1 - first)
+    return lax.switch(
+        choice,
+        [functools.partial(run, number) for number in range(len(choices))],
+        counts,
+        img,
+        cot,
+        gains,
+        depthwise,
+        pointwise,
+    )
 
 
 def solution(mesh):

time: 86.3 us -> 67.9 us (0.79)
  Pallas kernels: 79.3 us -> 60.1 us
  other arithmetic: 4.22 us -> 2.6 us
  between operations: 1.3 us -> 2.55 us
    pallas_call x1, Pallas kernels: 79.3 us -> 60.1 us  [run(): pl.pallas_call(functools.partial(kernel, plan), out_shape=(jax.ShapeDtype...]
    convert_element_type x1, other arithmetic: 4.22 us -> 2.6 us  [run(): return (point.astype(F32), depth.transpose(1, 0, 2), gain)]
  transfers between devices with their start and end apart: 0 -> 1, of which waited for: 0 -> 1; matrix products, arithmetic and copies ran while one was open for 0% -> 0% of each run, Pallas kernels for 0% -> 0%
where the time goes in v3:
time: 67.9 us; the launch traced here: 67.8 us
  Pallas kernels  60.1 us (89%)
  other arithmetic  2.6 us (4%)
  between operations  2.55 us (4%)
  local copies, waits for them, and re-layouts  1.23 us (2%)
    pallas_call x1, Pallas kernels, run(): pl.pallas_call(functools.partial(kernel, plan), out_shape=(jax.ShapeDtype...  60.1 us
    convert_element_type x1, other arithmetic, run(): return (point.astype(F32), depth.transpose(1, 0, 2), gain)  2.6 us
  transfers between devices with their start and end apart: 1, of which 1 were waited for; matrix products, arithmetic and copies ran while one was open for 0% of the time, Pallas kernels for 0%

profile of v3, /device:TPU:0, one launch (start us, length us, event | category | flops | bytes accessed | tf_op | source)
XLA Modules:
  0.0 67.8 jit_solution(12761807445941317734)
XLA Ops:
  0.6 0.5 collective-permute-start
  1.8 0.3 collective-permute-done
  3.4 60.6 %conditional.2 = (bf16[4,512,512]{2,1,0:T(8,128)(2,1)S(1)}, f32[4,9,512]{2,0,1:T(4,128)S(1)}, f32[4,512]{1,0:T(4,128)S(1)}) conditional(s32[]{:T(128)} %clamp.3, (f32[4,9,512]{2,0,1:T(4,128)}, bf16[2,256,512]{2,1,0:T(8,128)(2,1)}, bf16[2,256,512]{2,1,0:T(8,128)(2,1)}, s32[1]{0:T(128)}, f32[4,512]{1,0:T(4,128)}, ...), branch_computations={%region_0.1_spmd, %region_1.2_spmd, %region_2.3_spmd, %region_3.4_... | conditional | bytes 24
  3.4 60.1 %branch_3_fun.1 = (bf16[4,512,512]{2,1,0:T(8,128)(2,1)S(1)}, f32[9,4,512]{2,1,0:T(4,128)S(1)}, f32[4,512]{1,0:T(4,128)S(1)}) custom-call(bf16[2,256,512]{2,1,0:T(8,128)(2,1)} %get-tuple-element.115.img, bf16[2,256,512]{2,1,0:T(8,128)(2,1)} %get-tuple-element.116.cot, s32[1]{0:T(128)} %get-tuple-element.117.counts, f32[4,512]{1,0:T(4,128)} %get-tuple-element.118.gains, ...), custom_call_target="tpu_custom_call" | custom-call | tf_op jit(solution)/shard_map/cond/branch_3_fun/pallas_call | solution.py:612
  63.9 2.6 %convert_element_type.6 = f32[4,512,512]{2,1,0:T(8,128)} convert(bf16[4,512,512]{2,1,0:T(8,128)(2,1)S(1)} %get-tuple-element.157) | non-fusion elementwise | flops 1048576 | bytes 6291456 | tf_op jit(solution)/shard_map/cond/branch_0_fun/convert_element_type | solution.py:656
  66.5 0.6 copy.33
  67.2 0.6 copy.34
Async XLA Ops:
  0.6 1.5 %collective-permute-start = (s32[1]{0:T(128)}, s32[1]{0:T(128)}, u32[]{:S(2)}, u32[]{:S(2)}) collective-permute-start(s32[1]{0:T(128)} %param.15), channel_id=1, source_target_pairs={{0,16},{16,0},{1,17},{17,1},{2,18},{18,2},{3,19},{19,3},{4,20},{20... | collective-permute-start | bytes 20 | tf_op jit(solution)/shard_map/ppermute | solution.py:658
